TPU v7x, 256 devices: a whole 4x4x8 slice. The times are simulated.
256 devices in a mesh: head: 4 (over z_lo), ctx: 64 (over z_hi, x, y, core).
Axes of the slice: x: 4, y: 4, z: 8 (z_hi: 2, z_lo: 4; z = z_hi * 4 + z_lo), core: 2. Of those that a mesh axis runs over, the one named last changes fastest.
Arguments:
- query_rows: bfloat16 [24576, 5120], P(('ctx', 'head')), may hold values from -26 to 26
- key_rows: bfloat16 [24576, 5120], P(('ctx', 'head')), may hold values from -26 to 26
- value_rows: bfloat16 [24576, 5120], P(('ctx', 'head')), may hold values from -6 to 6
- block_mask: int32 [40, 192, 192], P('head', 'ctx'), may hold values from 0 to 1
- head_type: int32 [40], P('head'), may hold values from 0 to 1
Outputs:
- attended: bfloat16 [24576, 5120], P(('ctx', 'head'))
All inputs are finite; a program needn't handle non-finite values.
Results may differ from a plain program's by a relative error of at most 0.0044.
Values may be sent and summed in bfloat16 or wider, within the bound.
A program may use at most 64 MiB of HBM per device.

v0:
```python
import math

import jax
import jax.numpy as jnp
from jax import lax
from jax.sharding import PartitionSpec as P

BLOCK = 128


masked_score = -1e30


def passed_along(x, axis, by):
    length = lax.axis_size(axis)
    return lax.ppermute(x, axis, [(i, (i + by) % length) for i in range(length)])


def per_device(query_rows, key_rows, value_rows, block_mask, head_type):
    q_all, k_all, v_all = (
        lax.all_to_all(query_rows, "head", split_axis=1, concat_axis=0, tiled=True),
        lax.all_to_all(key_rows, "head", split_axis=1, concat_axis=0, tiled=True),
        lax.all_to_all(value_rows, "head", split_axis=1, concat_axis=0, tiled=True),
    )
    rows = q_all.shape[0]
    heads = head_type.shape[0]
    width = q_all.shape[1] // heads
    count = lax.axis_size("ctx")
    reach = min(4, count // 4)
    here = lax.axis_index("ctx")
    per_dev = rows // BLOCK
    scale = 1.0 / math.sqrt(width)
    limits = jnp.where(head_type == 1, reach * per_dev, per_dev).astype(jnp.int32)
    query_blocks = here * per_dev + jnp.arange(per_dev, dtype=jnp.int32)
    queries = q_all.reshape(rows, heads, width)

    def attend(carry, packed, source):
        best, total, accum = carry
        key_blocks = source * per_dev + jnp.arange(per_dev, dtype=jnp.int32)
        tile_mask = lax.dynamic_slice_in_dim(block_mask, source * per_dev, per_dev, 2)
        distance = jnp.abs(query_blocks[:, None] - key_blocks[None, :])
        allowed = ((tile_mask == 1) | (distance == 0)[None]) & (
            distance[None] <= limits[:, None, None]
        )
        keys = packed[0].reshape(rows, heads, width)
        values = packed[1].reshape(rows, heads, width)
        token_mask = jnp.broadcast_to(
            allowed[:, :, None, :, None], (heads, per_dev, BLOCK, per_dev, BLOCK)
        ).reshape(heads, rows, rows)
        scores = (
            jnp.einsum("qhd,khd->hqk", queries, keys, preferred_element_type=jnp.float32) * scale
        )
        scores = jnp.where(token_mask, scores, masked_score)
        new_best = jnp.maximum(best, jnp.max(scores, axis=2))
        raw = jnp.where(token_mask, jnp.exp(scores - new_best[:, :, None]), 0.0)
        factor = jnp.exp(best - new_best)
        total = total * factor + jnp.sum(raw, axis=2)
        accum = accum * factor[:, :, None] + jnp.einsum(
            "hqk,khd->hqd", raw.astype(jnp.bfloat16), values, preferred_element_type=jnp.float32
        )
        return (new_best, total, accum)

    start = (
        jnp.full((heads, rows), masked_score, jnp.float32),
        jnp.zeros((heads, rows), jnp.float32),
        jnp.zeros((heads, rows, width), jnp.float32),
    )
    paired = jnp.stack((k_all, v_all))
    farthest = passed_along(paired, "ctx", -reach)
    state = attend(start, farthest, jnp.mod(here + reach, count))

    def advance(current, moving, source):
        moving = passed_along(moving, "ctx", 1)
        return (attend(current, moving, jnp.mod(source, count)), moving)

    def turn(step, carry):
        current, moving = carry
        current, moving = advance(current, moving, here + reach - 2 * step - 1)
        current, moving = advance(current, moving, here + reach - 2 * step - 2)
        return (current, moving)

    state = lax.fori_loop(0, reach, turn, (state, farthest))[0]
    best, total, accum = state
    mixed = accum / total[:, :, None]
    mixed = jnp.transpose(mixed, (1, 0, 2)).reshape(rows, heads * width).astype(jnp.bfloat16)
    return lax.all_to_all(mixed, "head", split_axis=0, concat_axis=1, tiled=True)


def solution(mesh):
    placed = (
        P(("ctx", "head"), None),
        P(("ctx", "head"), None),
        P(("ctx", "head"), None),
        P("head", "ctx", None),
        P("head"),
    )
    return jax.shard_map(
        per_device, mesh=mesh, in_specs=placed, out_specs=P(("ctx", "head"), None), check_vma=False
    )
```

profile of v0, /device:TPU:32, one launch (start us, length us, event | category | flops | bytes accessed | tf_op | source)
XLA Modules:
  0.0 612.1 jit_solution(13885037609410490844)
XLA Ops:
  0.0 2.3 copy.156
  2.3 6.0 all-to-all-start
  8.4 21.0 %all-to-all-done = bf16[96,4,1280]{2,0,1:T(8,128)(2,1)S(1)} async-done(((bf16[96,4,1280]{2,0,1:T(8,128)(2,1)}), bf16[96,4,1280]{2,0,1:T(8,128)(2,1)S(1)}, u32[]{:S(2)}, u32[]{:S(2)}) %all-to-all-start) | async-done | bytes 983072 | tf_op jit(solution)/shard_map/all_to_all | solution.py:22
  29.3 28.0 %all_to_all.64 = bf16[96,4,1280]{2,0,1:T(8,128)(2,1)S(1)} all-to-all(bf16[96,4,1280]{2,0,1:T(8,128)(2,1)S(1)} %bitcast.78), channel_id=1, replica_groups=mesh['head'=4,'ctx'=64] {'head'}, dimensions={1} | all-to-all | bytes 1966080 | tf_op jit(solution)/shard_map/all_to_all | solution.py:23
  58.9 9.9 %collective-permute-start.2 = (bf16[2,384,1280]{2,1,0:T(8,128)(2,1)}, bf16[2,384,1280]{2,1,0:T(8,128)(2,1)}, u32[]{:S(2)}, u32[]{:S(2)}) collective-permute-start(bf16[2,384,1280]{2,1,0:T(8,128)(2,1)} %pad_maximum_fusion), channel_id=1, source_target_pairs={{0,60},{1,61},{2,62},{3,63},{4,0},{5,1},{6,2},{7,3},{8,4},{9,5},{1... | collective-permute-start | bytes 5898248 | tf_op jit(solution)/shard_map/ppermute | solution.py:16
  69.8 5.8 all-to-all-start.2
  77.2 4.5 reshape.244
  83.4 89.7 %all-to-all-done.2 = bf16[96,4,1280]{2,0,1:T(8,128)(2,1)} async-done(((bf16[96,4,1280]{2,0,1:T(8,128)(2,1)}), bf16[96,4,1280]{2,0,1:T(8,128)(2,1)}, u32[]{:S(2)}, u32[]{:S(2)}) %all-to-all-start.2) | async-done | bytes 983072 | tf_op jit(solution)/shard_map/all_to_all | solution.py:21
  173.1 3.4 copy.122
  176.5 2.6 reshape.245
  180.5 2.6 fusion.54
  183.0 2.3 copy.120
  185.3 2.5 fusion.32
  191.0 6.8 %fusion.41 = f32[10,384,128]{2,1,0:T(8,128)} fusion(bf16[384,10,128]{0,2,1:T(8,128)(2,1)S(1)} %bitcast.86, pred[10,384,384]{1,2,0:T(32,128)(4,1)S(1)} %copy.125, f32[10,384,384]{2,1,0:T(8,128)} %copy-done.1, f32[10,384]{1,0:T(8,128)S(1)} %broadcast_maximum_fusion, f32[10,384]{1,0:T(8,128)S(1)} %get-tuple-element.381), kind=kOutput, calls=%fused_computation.56 | convolution fusion | flops 385351680 | bytes 10352640 | tf_op jit(solution)/shard_map/hqk,khd->hqd/dot_general | solution.py:58
  197.8 4.0 copy.130
  201.8 366.1 %while.22 = (s32[]{:T(128)}, f32[10,384]{1,0:T(8,128)S(1)}, f32[10,384]{1,0:T(8,128)S(1)}, f32[10,384,128]{2,1,0:T(8,128)}, bf16[2,384,1280]{1,2,0:T(8,128)(2,1)...) while((s32[]{:T(128)}, f32[10,384]{1,0:T(8,128)S(1)}, ...), condition=%wide.region_7.8_spmd.clone, body=%wide.region_2.7_spmd.clone.sunk | while | flops 1550270336 | bytes 116400200 | solution.py:82
  201.9 34.2 %collective-permute-done = bf16[2,384,1280]{1,2,0:T(8,128)(2,1)} collective-permute-done((bf16[2,384,1280]{1,2,0:T(8,128)(2,1)}, bf16[2,384,1280]{1,2,0:T(8,128)(2,1)}, u32[]{:S(2)}, u32[]{:S(2)}) %collective-permute-start) | collective-permute-done | bytes 1966112 | tf_op jit(solution)/shard_map/while/body/eval_jaxpr/ppermute | solution.py:16
  237.4 4.5 reshape.251
  244.6 6.0 reshape.252
  250.7 2.9 copy.160
  253.6 1.8 fusion.92
  256.7 21.6 %collective-permute-done.1 = bf16[2,384,1280]{1,2,0:T(8,128)(2,1)} collective-permute-done((bf16[2,384,1280]{1,2,0:T(8,128)(2,1)}, bf16[2,384,1280]{1,2,0:T(8,128)(2,1)}, u32[]{:S(2)}, u32[]{:S(2)}) %collective-permute-start.1) | collective-permute-done | bytes 1966112 | tf_op jit(solution)/shard_map/while/body/eval_jaxpr/ppermute | solution.py:16
  283.0 2.4 fusion.97
  287.3 4.0 multiply_add_fusion.5
  292.7 32.5 %collective-permute-done = bf16[2,384,1280]{1,2,0:T(8,128)(2,1)} collective-permute-done((bf16[2,384,1280]{1,2,0:T(8,128)(2,1)}, bf16[2,384,1280]{1,2,0:T(8,128)(2,1)}, u32[]{:S(2)}, u32[]{:S(2)}) %collective-permute-start) | collective-permute-done | bytes 1966112 | tf_op jit(solution)/shard_map/while/body/eval_jaxpr/ppermute | solution.py:16
  326.6 4.5 reshape.251
  333.8 6.0 reshape.252
  339.8 2.9 copy.160
  342.7 1.8 fusion.92
  345.8 24.4 %collective-permute-done.1 = bf16[2,384,1280]{1,2,0:T(8,128)(2,1)} collective-permute-done((bf16[2,384,1280]{1,2,0:T(8,128)(2,1)}, bf16[2,384,1280]{1,2,0:T(8,128)(2,1)}, u32[]{:S(2)}, u32[]{:S(2)}) %collective-permute-start.1) | collective-permute-done | bytes 1966112 | tf_op jit(solution)/shard_map/while/body/eval_jaxpr/ppermute | solution.py:16
  375.1 2.4 fusion.97
  379.3 4.0 multiply_add_fusion.5
  384.7 32.5 %collective-permute-done = bf16[2,384,1280]{1,2,0:T(8,128)(2,1)} collective-permute-done((bf16[2,384,1280]{1,2,0:T(8,128)(2,1)}, bf16[2,384,1280]{1,2,0:T(8,128)(2,1)}, u32[]{:S(2)}, u32[]{:S(2)}) %collective-permute-start) | collective-permute-done | bytes 1966112 | tf_op jit(solution)/shard_map/while/body/eval_jaxpr/ppermute | solution.py:16
  418.6 4.5 reshape.251
  425.8 6.0 reshape.252
  431.9 2.9 copy.160
  437.9 23.6 %collective-permute-done.1 = bf16[2,384,1280]{1,2,0:T(8,128)(2,1)} collective-permute-done((bf16[2,384,1280]{1,2,0:T(8,128)(2,1)}, bf16[2,384,1280]{1,2,0:T(8,128)(2,1)}, u32[]{:S(2)}, u32[]{:S(2)}) %collective-permute-start.1) | collective-permute-done | bytes 1966112 | tf_op jit(solution)/shard_map/while/body/eval_jaxpr/ppermute | solution.py:16
  466.3 2.4 fusion.97
  470.5 4.0 multiply_add_fusion.5
  475.9 32.5 %collective-permute-done = bf16[2,384,1280]{1,2,0:T(8,128)(2,1)} collective-permute-done((bf16[2,384,1280]{1,2,0:T(8,128)(2,1)}, bf16[2,384,1280]{1,2,0:T(8,128)(2,1)}, u32[]{:S(2)}, u32[]{:S(2)}) %collective-permute-start) | collective-permute-done | bytes 1966112 | tf_op jit(solution)/shard_map/while/body/eval_jaxpr/ppermute | solution.py:16
  509.8 4.5 reshape.251
  517.0 6.0 reshape.252
  523.1 2.9 copy.160
  529.1 24.4 %collective-permute-done.1 = bf16[2,384,1280]{1,2,0:T(8,128)(2,1)} collective-permute-done((bf16[2,384,1280]{1,2,0:T(8,128)(2,1)}, bf16[2,384,1280]{1,2,0:T(8,128)(2,1)}, u32[]{:S(2)}, u32[]{:S(2)}) %collective-permute-start.1) | collective-permute-done | bytes 1966112 | tf_op jit(solution)/shard_map/while/body/eval_jaxpr/ppermute | solution.py:16
  558.3 2.4 fusion.97
  562.6 4.0 multiply_add_fusion.5
  568.0 2.1 fusion.44
  571.4 39.7 %all_to_all.65 = bf16[4,96,1280]{2,1,0:T(8,128)(2,1)S(1)} all-to-all(bf16[4,96,1280]{2,1,0:T(8,128)(2,1)S(1)} %reshape.248), channel_id=1, replica_groups=mesh['head'=4,'ctx'=64] {'head'}, dimensions={0} | all-to-all | bytes 1966080 | tf_op jit(solution)/shard_map/all_to_all | solution.py:86
  (131 shorter events, 69.1 us)
Async XLA Ops:
  0.0 8.3 %copy-start.5 = (bf16[96,5120]{1,0:T(8,128)(2,1)S(1)}, bf16[96,5120]{1,0:T(8,128)(2,1)}, u32[]{:S(2)}) copy-start(bf16[96,5120]{1,0:T(8,128)(2,1)} %param.9) | copy-start | bytes 2949124
  2.3 27.0 %all-to-all-start = ((bf16[96,4,1280]{2,0,1:T(8,128)(2,1)}), bf16[96,4,1280]{2,0,1:T(8,128)(2,1)S(1)}, u32[]{:S(2)}, u32[]{:S(2)}) async-start(bf16[96,4,1280]{2,0,1:T(8,128)(2,1)} %bitcast.53), calls=%async_computation | async-start | bytes 1966080 | tf_op jit(solution)/shard_map/all_to_all | solution.py:22
  29.3 39.4 %copy-start.6 = (bf16[96,5120]{1,0:T(8,128)(2,1)S(1)}, bf16[96,5120]{1,0:T(8,128)(2,1)}, u32[]{:S(2)}) copy-start(bf16[96,5120]{1,0:T(8,128)(2,1)} %param.7) | copy-start | bytes 2949124
  58.9 16.8 %copy-start.9 = (s32[10]{0:T(128)S(1)}, s32[10]{0:T(128)}, u32[]{:S(2)}) copy-start(s32[10]{0:T(128)} %param.11) | copy-start | bytes 124
  58.9 16.9 %copy-start.4 = (s32[10,3,192]{2,1,0:T(4,128)S(1)}, s32[10,3,192]{2,1,0:T(4,128)}, u32[]{:S(2)}) copy-start(s32[10,3,192]{2,1,0:T(4,128)} %param.10) | copy-start | bytes 69124
  58.9 121.6 %collective-permute-start.2 = (bf16[2,384,1280]{2,1,0:T(8,128)(2,1)}, bf16[2,384,1280]{2,1,0:T(8,128)(2,1)}, u32[]{:S(2)}, u32[]{:S(2)}) collective-permute-start(bf16[2,384,1280]{2,1,0:T(8,128)(2,1)} %pad_maximum_fusion), channel_id=1, source_target_pairs={{0,60},{1,61},{2,62},{3,63},{4,0},{5,1},{6,2},{7,3},{8,4},{9,5},{1... | collective-permute-start | bytes 5898248 | tf_op jit(solution)/shard_map/ppermute | solution.py:16
  69.8 103.3 %all-to-all-start.2 = ((bf16[96,4,1280]{2,0,1:T(8,128)(2,1)}), bf16[96,4,1280]{2,0,1:T(8,128)(2,1)}, u32[]{:S(2)}, u32[]{:S(2)}) async-start(bf16[96,4,1280]{2,0,1:T(8,128)(2,1)} %bitcast.51), calls=%async_computation.2 | async-start | bytes 1966080 | tf_op jit(solution)/shard_map/all_to_all | solution.py:21
  75.6 0.5 copy-start.7
  187.8 2.5 copy-start.1
  197.8 4.0 copy-start.8
  201.8 34.2 %collective-permute-start = (bf16[2,384,1280]{1,2,0:T(8,128)(2,1)}, bf16[2,384,1280]{1,2,0:T(8,128)(2,1)}, u32[]{:S(2)}, u32[]{:S(2)}) collective-permute-start(bf16[2,384,1280]{1,2,0:T(8,128)(2,1)} %get-tuple-element.513), channel_id=1, source_target_pairs={{0,1},{1,2},{2,3},{3,4},{4,5},{5,6},{6,7},{7,8},{8,9},{9,10},{10,1... | collective-permute-start | bytes 5898248 | tf_op jit(solution)/shard_map/while/body/eval_jaxpr/ppermute | solution.py:16
  236.0 42.2 %collective-permute-start.1 = (bf16[2,384,1280]{1,2,0:T(8,128)(2,1)}, bf16[2,384,1280]{1,2,0:T(8,128)(2,1)}, u32[]{:S(2)}, u32[]{:S(2)}) collective-permute-start(bf16[2,384,1280]{1,2,0:T(8,128)(2,1)} %collective-permute-done), channel_id=1, source_target_pairs={{0,1},{1,2},{2,3},{3,4},{4,5},{5,6},{6,7},{7,8},{8,9},{9,10},{10,1... | collective-permute-start | bytes 5898248 | tf_op jit(solution)/shard_map/while/body/eval_jaxpr/ppermute | solution.py:16
  253.6 1.8 copy-start
  285.5 1.8 copy-start.2
  291.3 1.4 copy-start.3
  292.7 32.5 %collective-permute-start = (bf16[2,384,1280]{1,2,0:T(8,128)(2,1)}, bf16[2,384,1280]{1,2,0:T(8,128)(2,1)}, u32[]{:S(2)}, u32[]{:S(2)}) collective-permute-start(bf16[2,384,1280]{1,2,0:T(8,128)(2,1)} %get-tuple-element.513), channel_id=1, source_target_pairs={{0,1},{1,2},{2,3},{3,4},{4,5},{5,6},{6,7},{7,8},{8,9},{9,10},{10,1... | collective-permute-start | bytes 5898248 | tf_op jit(solution)/shard_map/while/body/eval_jaxpr/ppermute | solution.py:16
  325.2 45.1 %collective-permute-start.1 = (bf16[2,384,1280]{1,2,0:T(8,128)(2,1)}, bf16[2,384,1280]{1,2,0:T(8,128)(2,1)}, u32[]{:S(2)}, u32[]{:S(2)}) collective-permute-start(bf16[2,384,1280]{1,2,0:T(8,128)(2,1)} %collective-permute-done), channel_id=1, source_target_pairs={{0,1},{1,2},{2,3},{3,4},{4,5},{5,6},{6,7},{7,8},{8,9},{9,10},{10,1... | collective-permute-start | bytes 5898248 | tf_op jit(solution)/shard_map/while/body/eval_jaxpr/ppermute | solution.py:16
  342.7 1.8 copy-start
  377.5 1.8 copy-start.2
  383.4 1.4 copy-start.3
  384.7 32.5 %collective-permute-start = (bf16[2,384,1280]{1,2,0:T(8,128)(2,1)}, bf16[2,384,1280]{1,2,0:T(8,128)(2,1)}, u32[]{:S(2)}, u32[]{:S(2)}) collective-permute-start(bf16[2,384,1280]{1,2,0:T(8,128)(2,1)} %get-tuple-element.513), channel_id=1, source_target_pairs={{0,1},{1,2},{2,3},{3,4},{4,5},{5,6},{6,7},{7,8},{8,9},{9,10},{10,1... | collective-permute-start | bytes 5898248 | tf_op jit(solution)/shard_map/while/body/eval_jaxpr/ppermute | solution.py:16
  417.2 44.3 %collective-permute-start.1 = (bf16[2,384,1280]{1,2,0:T(8,128)(2,1)}, bf16[2,384,1280]{1,2,0:T(8,128)(2,1)}, u32[]{:S(2)}, u32[]{:S(2)}) collective-permute-start(bf16[2,384,1280]{1,2,0:T(8,128)(2,1)} %collective-permute-done), channel_id=1, source_target_pairs={{0,1},{1,2},{2,3},{3,4},{4,5},{5,6},{6,7},{7,8},{8,9},{9,10},{10,1... | collective-permute-start | bytes 5898248 | tf_op jit(solution)/shard_map/while/body/eval_jaxpr/ppermute | solution.py:16
  434.8 1.8 copy-start
  468.7 1.8 copy-start.2
  474.6 1.4 copy-start.3
  475.9 32.5 %collective-permute-start = (bf16[2,384,1280]{1,2,0:T(8,128)(2,1)}, bf16[2,384,1280]{1,2,0:T(8,128)(2,1)}, u32[]{:S(2)}, u32[]{:S(2)}) collective-permute-start(bf16[2,384,1280]{1,2,0:T(8,128)(2,1)} %get-tuple-element.513), channel_id=1, source_target_pairs={{0,1},{1,2},{2,3},{3,4},{4,5},{5,6},{6,7},{7,8},{8,9},{9,10},{10,1... | collective-permute-start | bytes 5898248 | tf_op jit(solution)/shard_map/while/body/eval_jaxpr/ppermute | solution.py:16
  508.4 45.1 %collective-permute-start.1 = (bf16[2,384,1280]{1,2,0:T(8,128)(2,1)}, bf16[2,384,1280]{1,2,0:T(8,128)(2,1)}, u32[]{:S(2)}, u32[]{:S(2)}) collective-permute-start(bf16[2,384,1280]{1,2,0:T(8,128)(2,1)} %collective-permute-done), channel_id=1, source_target_pairs={{0,1},{1,2},{2,3},{3,4},{4,5},{5,6},{6,7},{7,8},{8,9},{9,10},{10,1... | collective-permute-start | bytes 5898248 | tf_op jit(solution)/shard_map/while/body/eval_jaxpr/ppermute | solution.py:16
  526.0 1.8 copy-start
  560.7 1.8 copy-start.2
  566.6 1.4 copy-start.3
where the time goes:
time: 613 us; the launch traced here: 612 us
  waiting for transfers between devices  336 us (55%)
  local copies, waits for them, and re-layouts  119 us (19%)
  blocking collectives  67.7 us (11%)
  matrix products  45.6 us (7%)
  starting transfers between devices  21.8 us (4%)
  other arithmetic  20.9 us (3%)
    ppermute x9, waiting for transfers between devices, passed_along(): lax.ppermute(x, axis, [(i, (i + by) % length) for i in range(length)])  226 us
    all_to_all x1, waiting for transfers between devices, per_device(): lax.all_to_all(query_rows, 'head', split_axis=1, concat_axis=0, tiled=True)  89.7 us
    reshape x18, local copies, waits for them, and re-layouts, attend(): token_mask = jnp.broadcast_to(allowed[:, :, None, :, None], (heads, per_d...  66.4 us
    all_to_all x1, blocking collectives, per_device(): lax.all_to_all(mixed, 'head', split_axis=0, concat_axis=1, tiled=True)  39.7 us
    dot_general x9, matrix products, attend(): jnp.einsum('hqk,khd->hqd', raw.astype(jnp.bfloat16), values, preferred_el...  32.6 us
    all_to_all x1, blocking collectives, per_device(): lax.all_to_all(value_rows, 'head', split_axis=1, concat_axis=0, tiled=True)  28 us
    all_to_all x1, waiting for transfers between devices, per_device(): lax.all_to_all(key_rows, 'head', split_axis=1, concat_axis=0, tiled=True)  21 us
    slice x10, local copies, waits for them, and re-layouts, attend(): values = packed[1].reshape(rows, heads, width)  17.1 us
  transfers between devices with their start and end apart: 11, of which 10 were waited for; matrix products, arithmetic and copies ran while one was open for 16% of the time, Pallas kernels for 0%

commit v1 on v0

v1 whole, which is shorter than its diff:
```python
import math

import jax
import jax.numpy as jnp
from jax import lax
from jax.experimental import pallas as pl
from jax.experimental.pallas import tpu as pltpu
from jax.sharding import PartitionSpec as P

MESH = pl.DeviceIdType.MESH
TILE = 128
DIM = 128
HEADS = 5
ROWS = 96
CHUNK = 768
TILES = CHUNK // TILE
REACH = 12
NEAR = 3
SPAN = 2 * REACH + 1
KEYS = SPAN * TILE
WINDOW = 5 * CHUNK
OWN = 2 * CHUNK
CHUNKS = 32
FLAG_ROWS = 16
LOW = 1e30
RATE = math.log2(math.e) / math.sqrt(DIM)


def wait_for(ref, sem):
    pltpu.make_async_copy(ref, ref, sem).wait()


def kernel(
    q_ref, k_ref, v_ref, flag_ref, o_ref,
    kv, qb, ob, flags, bias,
    kv_send, q_send, flag_send, o_send, y_send,
    kv_recv, q_recv, flag_recv, o_recv, near_recv, far_recv,
):
    hd = lax.axis_index("head")
    ctx = lax.axis_index("ctx")
    zh = ctx // 32
    xy = (ctx // 2) % 16
    core = ctx % 2
    z = zh * 4 + hd
    chunk = core * 16 + xy
    loops = zh == core
    has_left = chunk > 0
    has_right = chunk < CHUNKS - 1

    def at(z_, xy_, core_):
        return {"head": z_ % 4, "ctx": (z_ // 4) * 32 + xy_ * 2 + core_}

    left = at(z, (chunk + CHUNKS - 1) % 16, ((chunk + CHUNKS - 1) % CHUNKS) // 16)
    right = at(z, (chunk + 1) % 16, ((chunk + 1) % CHUNKS) // 16)

    barrier = pltpu.get_barrier_semaphore()

    def greet(n, carry):
        other = (z * 2 + core + n) % 16
        pl.semaphore_signal(barrier, inc=1, device_id=at(other // 2, xy, other % 2), device_id_type=MESH)
        return carry

    lax.fori_loop(1, 16, greet, 0)

    @pl.when(has_left)
    def _():
        pl.semaphore_signal(barrier, inc=1, device_id=left, device_id_type=MESH)

    @pl.when(has_right)
    def _():
        pl.semaphore_signal(barrier, inc=1, device_id=right, device_id_type=MESH)

    pl.semaphore_wait(barrier, 15 + has_left.astype(jnp.int32) + has_right.astype(jnp.int32))

    mine = core * 384 + hd * ROWS

    def parts(i, z_):
        cols = pl.ds(pl.multiple_of((z_ * HEADS + i) * DIM, DIM), DIM)
        rows = pl.ds(pl.multiple_of(OWN + mine, 16), ROWS)
        q_rows = pl.ds(pl.multiple_of(mine, 16), ROWS)
        return (
            (k_ref.at[:, cols], kv.at[i, 0, rows, :], kv_send, kv_recv.at[i]),
            (v_ref.at[:, cols], kv.at[i, 1, rows, :], kv_send, kv_recv.at[i]),
            (q_ref.at[:, cols], qb.at[i, q_rows, :], q_send, q_recv.at[i]),
        )

    def push(src, dst, send, recv, to):
        pltpu.make_async_remote_copy(
            src_ref=src, dst_ref=dst, send_sem=send, recv_sem=recv, device_id=to, device_id_type=MESH
        ).start()

    def spread(i, carry):
        def one(j, inner):
            half = j // 2 + 1
            step = jnp.where(j % 2 == 0, half, 8 - half)
            z_ = (z + step) % 8
            for src, dst, send, recv in parts(i, z_):
                push(src, dst, send, recv, at(z_, xy, zh))
            return inner

        lax.fori_loop(0, 7, one, 0)

        @pl.when(loops)
        def _():
            for src, dst, send, recv in parts(i, z):
                pltpu.make_async_copy(src, dst, recv).start()

        @pl.when(jnp.logical_not(loops))
        def _():
            for src, dst, send, recv in parts(i, z):
                push(src, dst, send, recv, at(z, xy, zh))

        return carry

    lax.fori_loop(0, HEADS, spread, 0)

    for e in range(2):
        z_ = 2 * hd + e
        here = jnp.logical_and(loops, z_ == z)

        @pl.when(here)
        def _():
            pltpu.make_async_copy(flag_ref.at[e], flags.at[core], flag_recv).start()

        @pl.when(jnp.logical_not(here))
        def _():
            push(flag_ref.at[e], flags.at[core], flag_send.at[e], flag_recv, at(z_, xy, zh))

    def clear(slot, when):
        @pl.when(when)
        def _():
            def one(i, carry):
                kv[i, :, pl.ds(slot * CHUNK, CHUNK), :] = jnp.zeros((2, CHUNK, DIM), jnp.bfloat16)
                return carry

            lax.fori_loop(0, HEADS, one, 0)

    clear(0, chunk < 2)
    clear(1, chunk < 1)
    clear(3, chunk > CHUNKS - 2)
    clear(4, chunk > CHUNKS - 3)

    wait_for(flags, flag_recv)
    spots = lax.broadcasted_iota(jnp.int32, (TILE, KEYS), 1) // TILE
    rows_ = lax.broadcasted_iota(jnp.int32, (TILE, KEYS), 0)
    wide = (spots == rows_).astype(jnp.bfloat16)
    for c in range(2):
        seen = jnp.dot(flags[c].astype(jnp.bfloat16), wide, preferred_element_type=jnp.float32)
        bias[c] = (seen - 1.0) * LOW

    def slot(i, s):
        return kv.at[i, :, pl.ds(s * CHUNK, CHUNK), :]

    def send_own(i):
        wait_for(slot(i, 2), kv_recv.at[i])

        @pl.when(has_right)
        def _():
            push(slot(i, 2), slot(i, 1), y_send.at[0], near_recv.at[0, i], right)

        @pl.when(has_left)
        def _():
            push(slot(i, 2), slot(i, 3), y_send.at[1], near_recv.at[1, i], left)

    def pass_on(i):
        @pl.when(has_left)
        def _():
            wait_for(slot(i, 1), near_recv.at[0, i])

            @pl.when(has_right)
            def _():
                push(slot(i, 1), slot(i, 0), y_send.at[2], far_recv.at[0, i], right)

        @pl.when(has_right)
        def _():
            wait_for(slot(i, 3), near_recv.at[1, i])

            @pl.when(has_left)
            def _():
                push(slot(i, 3), slot(i, 4), y_send.at[3], far_recv.at[1, i], left)

    def attend(i):
        wait_for(qb.at[i], q_recv.at[i])

        @pl.when(chunk >= 2)
        def _():
            wait_for(slot(i, 0), far_recv.at[0, i])

        @pl.when(chunk < CHUNKS - 2)
        def _():
            wait_for(slot(i, 4), far_recv.at[1, i])

        def tile(a, carry):
            start = pl.multiple_of(a * TILE, TILE)
            q = qb[i, pl.ds(start, TILE), :]
            keys = kv[i, 0, pl.ds(start, KEYS), :]
            s = lax.dot_general(q, keys, (((1,), (1,)), ((), ())), preferred_element_type=jnp.float32)
            s = s + bias[a // 3, pl.ds(i * 3 + a % 3, 1), :]
            best = jnp.max(s, axis=1, keepdims=True)
            raw = jnp.exp2((s - best) * RATE)
            total = jnp.sum(raw, axis=1, keepdims=True)
            values = kv[i, 1, pl.ds(start, KEYS), :]
            mixed = jnp.dot(raw.astype(jnp.bfloat16), values, preferred_element_type=jnp.float32)
            ob[i, pl.ds(start, TILE), :] = (mixed / total).astype(jnp.bfloat16)
            return carry

        lax.fori_loop(0, TILES, tile, 0)

        cols = pl.ds(pl.multiple_of((z * HEADS + i) * DIM, DIM), DIM)

        def owner(n):
            zl = (hd + n // 2) % 4
            cs = (core + n) % 2
            return ob.at[i, pl.ds(pl.multiple_of(cs * 384 + zl * ROWS, 16), ROWS), :], at(core * 4 + zl, xy, cs)

        @pl.when(loops)
        def _():
            pltpu.make_async_copy(owner(0)[0], o_ref.at[:, cols], o_recv).start()

        @pl.when(jnp.logical_not(loops))
        def _():
            push(owner(0)[0], o_ref.at[:, cols], o_send, o_recv, owner(0)[1])

        def one(n, carry):
            src, to = owner(n)
            push(src, o_ref.at[:, cols], o_send, o_recv, to)
            return carry

        lax.fori_loop(1, 8, one, 0)

    for step in range(HEADS + 2):
        if step < HEADS:
            send_own(step)
        if 1 <= step <= HEADS:
            pass_on(step - 1)
        if step >= 2:
            attend(step - 2)

    wait_for(o_ref, o_recv)

    def sent(rows):
        wait_for(kv.at[:, :, pl.ds(0, rows), :], kv_send)
        wait_for(qb.at[:, pl.ds(0, rows), :], q_send)
        wait_for(ob.at[:, pl.ds(0, rows), :], o_send)

    @pl.when(loops)
    def _():
        sent(CHUNK - ROWS)

    @pl.when(jnp.logical_not(loops))
    def _():
        sent(CHUNK)

    for e in range(2):

        @pl.when(jnp.logical_not(jnp.logical_and(loops, 2 * hd + e == z)))
        def _():
            wait_for(flag_ref.at[e], flag_send.at[e])

    whole = kv.at[:, :, pl.ds(0, CHUNK), :]

    @pl.when(has_right)
    def _():
        wait_for(whole, y_send.at[0])

        @pl.when(has_left)
        def _():
            wait_for(whole, y_send.at[2])

    @pl.when(has_left)
    def _():
        wait_for(whole, y_send.at[1])

        @pl.when(has_right)
        def _():
            wait_for(whole, y_send.at[3])


def per_device(query_rows, key_rows, value_rows, block_mask, head_type):
    ctx = lax.axis_index("ctx")
    heads, tiles, count = block_mask.shape
    padded = jnp.pad(block_mask, ((0, 0), (0, 0), (REACH, REACH)))
    near = lax.dynamic_slice_in_dim(padded, ctx * tiles, SPAN + tiles - 1, 2)
    seen = jnp.stack([near[:, t, t : t + SPAN] for t in range(tiles)], axis=1)
    distance = jnp.abs(jnp.arange(SPAN, dtype=jnp.int32) - REACH)
    limit = jnp.where(head_type == 1, REACH, NEAR).astype(jnp.int32)
    allowed = ((seen == 1) | (distance == 0)) & (distance <= limit[:, None, None])
    flags = allowed.astype(jnp.float32).reshape(2, HEADS * tiles, SPAN)
    flags = jnp.pad(flags, ((0, 0), (0, FLAG_ROWS - HEADS * tiles), (0, TILE - SPAN)))
    any_ = pl.BlockSpec(memory_space=pl.ANY)
    dma = pltpu.SemaphoreType.DMA
    return pl.pallas_call(
        kernel,
        out_shape=jax.ShapeDtypeStruct(query_rows.shape, jnp.bfloat16),
        in_specs=[any_] * 4,
        out_specs=any_,
        scratch_shapes=[
            pltpu.VMEM((HEADS, 2, WINDOW, DIM), jnp.bfloat16),
            pltpu.VMEM((HEADS, CHUNK, DIM), jnp.bfloat16),
            pltpu.VMEM((HEADS, CHUNK, DIM), jnp.bfloat16),
            pltpu.VMEM((2, FLAG_ROWS, TILE), jnp.float32),
            pltpu.VMEM((2, FLAG_ROWS, KEYS), jnp.float32),
            dma, dma, dma((2,)), dma, dma((4,)),
            dma((HEADS,)), dma((HEADS,)), dma, dma, dma((2, HEADS)), dma((2, HEADS)),
        ],
        compiler_params=pltpu.CompilerParams(
            collective_id=0, has_side_effects=True, vmem_limit_bytes=48 * 1024 * 1024
        ),
    )(query_rows, key_rows, value_rows, flags)


def solution(mesh):
    placed = (
        P(("ctx", "head"), None),
        P(("ctx", "head"), None),
        P(("ctx", "head"), None),
        P("head", "ctx", None),
        P("head"),
    )
    return jax.shard_map(
        per_device, mesh=mesh, in_specs=placed, out_specs=P(("ctx", "head"), None), check_vma=False
    )
```

time: 613 us -> 178 us (0.29)
  the two profiles are of different devices: /device:TPU:32 before, /device:TPU:11 now
where the time goes in v1:
time: 178 us; the launch traced here: 177 us
  Pallas kernels  171 us (96%)
  local copies, waits for them, and re-layouts  4.74 us (3%)
    pallas_call x1, Pallas kernels, per_device(): pl.pallas_call(kernel, out_shape=jax.ShapeDtypeStruct(query_rows.shape, j...  171 us
    unnamed x9, local copies, waits for them, and re-layouts  4.55 us

profile of v1, /device:TPU:11, one launch (start us, length us, event | category | flops | bytes accessed | tf_op | source)
XLA Modules:
  0.0 176.6 jit_solution(866480187779885512)
XLA Ops:
  0.0 0.0 copy-start.3
  0.0 0.7 compare_select_fusion
  0.7 0.1 broadcast_compare_fusion
  0.8 0.0 copy-done.3
  0.8 0.1 pad_dynamic-slice_fusion.1
  1.0 0.0 copy-start
  1.0 1.2 copy-done
  2.2 0.0 copy-start.1
  2.2 1.2 copy-done.1
  3.4 0.0 copy-start.2
  3.4 1.2 copy-done.2
  4.6 171.0 %shard_map.55 = bf16[96,5120]{1,0:T(8,128)(2,1)S(1)} custom-call(bf16[96,5120]{1,0:T(8,128)(2,1)S(1)} %copy-done, bf16[96,5120]{1,0:T(8,128)(2,1)S(1)} %copy-done.1, bf16[96,5120]{1,0:T(8,128)(2,1)S(1)} %copy-done.2, f32[2,16,128]{2,1,0:T(8,128)S(1)} %pad_convert_fusion.flag_ref), custom_call_target="tpu_custom_call" | custom-call | tf_op jit(solution)/shard_map/pallas_call | solution.py:292
  175.6 0.9 copy.7
  (8 shorter events, 0.1 us)
Async XLA Ops:
  0.0 0.8 copy-start.3
  1.0 1.2 copy-start
  2.2 1.2 copy-start.1
  3.4 1.2 copy-start.2

commit v2 on v1

--- a/solution.py
+++ b/solution.py
@@ -16,8 +16,11 @@
 TILES = CHUNK // TILE
 REACH = 12
 NEAR = 3
-SPAN = 2 * REACH + 1
+PAIR = 2 * TILE
+SPAN = 2 * REACH + 2
 KEYS = SPAN * TILE
+STEP = 256
+UNITS = 2 * HEADS
 WINDOW = 5 * CHUNK
 OWN = 2 * CHUNK
 CHUNKS = 32
@@ -32,7 +35,7 @@
 
 def kernel(
     q_ref, k_ref, v_ref, flag_ref, o_ref,
-    kv, qb, ob, flags, bias,
+    kv, qb, ob, flags, bias, held,
     kv_send, q_send, flag_send, o_send, y_send,
     kv_recv, q_recv, flag_recv, o_recv, near_recv, far_recv,
 ):
@@ -79,8 +82,8 @@
         rows = pl.ds(pl.multiple_of(OWN + mine, 16), ROWS)
         q_rows = pl.ds(pl.multiple_of(mine, 16), ROWS)
         return (
-            (k_ref.at[:, cols], kv.at[i, 0, rows, :], kv_send, kv_recv.at[i]),
-            (v_ref.at[:, cols], kv.at[i, 1, rows, :], kv_send, kv_recv.at[i]),
+            (k_ref.at[:, cols], kv.at[2 * i, rows, :], kv_send, kv_recv.at[2 * i]),
+            (v_ref.at[:, cols], kv.at[2 * i + 1, rows, :], kv_send, kv_recv.at[2 * i + 1]),
             (q_ref.at[:, cols], qb.at[i, q_rows, :], q_send, q_recv.at[i]),
         )
 
@@ -89,30 +92,29 @@
             src_ref=src, dst_ref=dst, send_sem=send, recv_sem=recv, device_id=to, device_id_type=MESH
         ).start()
 
-    def spread(i, carry):
-        def one(j, inner):
+    def spread(i, kind):
+        def one(j, carry):
             half = j // 2 + 1
             step = jnp.where(j % 2 == 0, half, 8 - half)
             z_ = (z + step) % 8
-            for src, dst, send, recv in parts(i, z_):
-                push(src, dst, send, recv, at(z_, xy, zh))
-            return inner
+            src, dst, send, recv = parts(i, z_)[kind]
+            push(src, dst, send, recv, at(z_, xy, zh))
+            return carry
 
         lax.fori_loop(0, 7, one, 0)
 
         @pl.when(loops)
         def _():
-            for src, dst, send, recv in parts(i, z):
-                pltpu.make_async_copy(src, dst, recv).start()
+            src, dst, send, recv = parts(i, z)[kind]
+            pltpu.make_async_copy(src, dst, recv).start()
 
         @pl.when(jnp.logical_not(loops))
         def _():
-            for src, dst, send, recv in parts(i, z):
-                push(src, dst, send, recv, at(z, xy, zh))
-
-        return carry
-
-    lax.fori_loop(0, HEADS, spread, 0)
+            src, dst, send, recv = parts(i, z)[kind]
+            push(src, dst, send, recv, at(z, xy, zh))
+
+    spread(0, 0)
+    spread(0, 1)
 
     for e in range(2):
         z_ = 2 * hd + e
@@ -130,10 +132,10 @@
         @pl.when(when)
         def _():
             def one(i, carry):
-                kv[i, :, pl.ds(slot * CHUNK, CHUNK), :] = jnp.zeros((2, CHUNK, DIM), jnp.bfloat16)
+                kv[i, pl.ds(slot * CHUNK, CHUNK), :] = jnp.zeros((CHUNK, DIM), jnp.bfloat16)
                 return carry
 
-            lax.fori_loop(0, HEADS, one, 0)
+            lax.fori_loop(0, UNITS, one, 0)
 
     clear(0, chunk < 2)
     clear(1, chunk < 1)
@@ -146,10 +148,12 @@
     wide = (spots == rows_).astype(jnp.bfloat16)
     for c in range(2):
         seen = jnp.dot(flags[c].astype(jnp.bfloat16), wide, preferred_element_type=jnp.float32)
-        bias[c] = (seen - 1.0) * LOW
+        seen = (seen - 1.0) * LOW
+        for i in range(HEADS):
+            bias[pl.ds(i * TILES + 3 * c, 3), :] = seen[3 * i : 3 * i + 3]
 
     def slot(i, s):
-        return kv.at[i, :, pl.ds(s * CHUNK, CHUNK), :]
+        return kv.at[i, pl.ds(s * CHUNK, CHUNK), :]
 
     def send_own(i):
         wait_for(slot(i, 2), kv_recv.at[i])
@@ -181,30 +185,40 @@
 
     def attend(i):
         wait_for(qb.at[i], q_recv.at[i])
-
-        @pl.when(chunk >= 2)
-        def _():
-            wait_for(slot(i, 0), far_recv.at[0, i])
-
-        @pl.when(chunk < CHUNKS - 2)
-        def _():
-            wait_for(slot(i, 4), far_recv.at[1, i])
-
-        def tile(a, carry):
-            start = pl.multiple_of(a * TILE, TILE)
-            q = qb[i, pl.ds(start, TILE), :]
-            keys = kv[i, 0, pl.ds(start, KEYS), :]
-            s = lax.dot_general(q, keys, (((1,), (1,)), ((), ())), preferred_element_type=jnp.float32)
-            s = s + bias[a // 3, pl.ds(i * 3 + a % 3, 1), :]
-            best = jnp.max(s, axis=1, keepdims=True)
-            raw = jnp.exp2((s - best) * RATE)
-            total = jnp.sum(raw, axis=1, keepdims=True)
-            values = kv[i, 1, pl.ds(start, KEYS), :]
-            mixed = jnp.dot(raw.astype(jnp.bfloat16), values, preferred_element_type=jnp.float32)
-            ob[i, pl.ds(start, TILE), :] = (mixed / total).astype(jnp.bfloat16)
-            return carry
-
-        lax.fori_loop(0, TILES, tile, 0)
+        for u in (2 * i, 2 * i + 1):
+
+            @pl.when(chunk >= 2)
+            def _():
+                wait_for(slot(u, 0), far_recv.at[0, u])
+
+            @pl.when(chunk < CHUNKS - 2)
+            def _():
+                wait_for(slot(u, 4), far_recv.at[1, u])
+
+        for p in range(CHUNK // PAIR):
+            start = p * PAIR
+            q = qb[i, pl.ds(start, PAIR), :]
+            best = jnp.full((PAIR, TILE), -3e38, jnp.float32)
+            for j in range(0, KEYS, STEP):
+                keys = kv[2 * i, pl.ds(start + j, STEP), :]
+                s = lax.dot_general(q, keys, (((1,), (1,)), ((), ())), preferred_element_type=jnp.float32)
+                even = s[:TILE] + bias[pl.ds(i * TILES + 2 * p, 1), pl.ds(j, STEP)]
+                odd = s[TILE:] + bias[pl.ds(i * TILES + 2 * p + 1, 1), pl.ds(j, STEP)]
+                s = jnp.concatenate([even, odd], axis=0)
+                held[p, :, pl.ds(j, STEP)] = s
+                for t in range(0, STEP, TILE):
+                    best = jnp.maximum(best, s[:, t : t + TILE])
+            best = jnp.max(best, axis=1, keepdims=True)
+            total = jnp.zeros((PAIR, TILE), jnp.float32)
+            mixed = jnp.zeros((PAIR, DIM), jnp.float32)
+            for j in range(0, KEYS, STEP):
+                raw = jnp.exp2((held[p, :, pl.ds(j, STEP)] - best) * RATE)
+                for t in range(0, STEP, TILE):
+                    total = total + raw[:, t : t + TILE]
+                values = kv[2 * i + 1, pl.ds(start + j, STEP), :]
+                mixed = mixed + jnp.dot(raw.astype(jnp.bfloat16), values, preferred_element_type=jnp.float32)
+            total = jnp.sum(total, axis=1, keepdims=True)
+            ob[i, pl.ds(start, PAIR), :] = (mixed / total).astype(jnp.bfloat16)
 
         cols = pl.ds(pl.multiple_of((z * HEADS + i) * DIM, DIM), DIM)
 
@@ -228,18 +242,49 @@
 
         lax.fori_loop(1, 8, one, 0)
 
-    for step in range(HEADS + 2):
-        if step < HEADS:
-            send_own(step)
-        if 1 <= step <= HEADS:
-            pass_on(step - 1)
-        if step >= 2:
-            attend(step - 2)
+    def advance(s, carry):
+        @pl.when(s < HEADS)
+        def _():
+            for t in range(2):
+                send_own(2 * s + t)
+
+                @pl.when(s < HEADS - 1)
+                def _():
+                    spread(s + 1, t)
+
+                if t == 1:
+
+                    @pl.when(s >= 1)
+                    def _():
+                        spread(s - 1, 2)
+
+                    @pl.when(s == HEADS - 1)
+                    def _():
+                        spread(s, 2)
+
+                    pass_on(2 * s)
+                else:
+
+                    @pl.when(s >= 1)
+                    def _():
+                        pass_on(2 * s - 1)
+
+        @pl.when(s == HEADS)
+        def _():
+            pass_on(UNITS - 1)
+
+        @pl.when(s >= 2)
+        def _():
+            attend(s - 2)
+
+        return carry
+
+    lax.fori_loop(0, HEADS + 2, advance, 0)
 
     wait_for(o_ref, o_recv)
 
     def sent(rows):
-        wait_for(kv.at[:, :, pl.ds(0, rows), :], kv_send)
+        wait_for(kv.at[:, pl.ds(0, rows), :], kv_send)
         wait_for(qb.at[:, pl.ds(0, rows), :], q_send)
         wait_for(ob.at[:, pl.ds(0, rows), :], o_send)
 
@@ -257,7 +302,7 @@
         def _():
             wait_for(flag_ref.at[e], flag_send.at[e])
 
-    whole = kv.at[:, :, pl.ds(0, CHUNK), :]
+    whole = kv.at[:, pl.ds(0, CHUNK), :]
 
     @pl.when(has_right)
     def _():
@@ -279,15 +324,20 @@
 def per_device(query_rows, key_rows, value_rows, block_mask, head_type):
     ctx = lax.axis_index("ctx")
     heads, tiles, count = block_mask.shape
-    padded = jnp.pad(block_mask, ((0, 0), (0, 0), (REACH, REACH)))
-    near = lax.dynamic_slice_in_dim(padded, ctx * tiles, SPAN + tiles - 1, 2)
-    seen = jnp.stack([near[:, t, t : t + SPAN] for t in range(tiles)], axis=1)
-    distance = jnp.abs(jnp.arange(SPAN, dtype=jnp.int32) - REACH)
+    padded = jnp.pad(block_mask, ((0, 0), (0, 0), (REACH + 1, REACH + 1)))
+    base = ctx * tiles
+    shift = (base + jnp.arange(tiles, dtype=jnp.int32)) % 2
+    near = lax.dynamic_slice_in_dim(padded, base, SPAN + tiles, 2)
+    seen = jnp.stack(
+        [jnp.where(shift[t] == 1, near[:, t, t : t + SPAN], near[:, t, t + 1 : t + 1 + SPAN]) for t in range(tiles)],
+        axis=1,
+    )
+    distance = jnp.abs(jnp.arange(SPAN, dtype=jnp.int32) - REACH - shift[:, None])
     limit = jnp.where(head_type == 1, REACH, NEAR).astype(jnp.int32)
     allowed = ((seen == 1) | (distance == 0)) & (distance <= limit[:, None, None])
     flags = allowed.astype(jnp.float32).reshape(2, HEADS * tiles, SPAN)
     flags = jnp.pad(flags, ((0, 0), (0, FLAG_ROWS - HEADS * tiles), (0, TILE - SPAN)))
-    any_ = pl.BlockSpec(memory_space=pl.ANY)
+    any_ = pl.BlockSpec(memory_space=pltpu.HBM)
     dma = pltpu.SemaphoreType.DMA
     return pl.pallas_call(
         kernel,
@@ -295,16 +345,17 @@
         in_specs=[any_] * 4,
         out_specs=any_,
         scratch_shapes=[
-            pltpu.VMEM((HEADS, 2, WINDOW, DIM), jnp.bfloat16),
+            pltpu.VMEM((UNITS, WINDOW, DIM), jnp.bfloat16),
             pltpu.VMEM((HEADS, CHUNK, DIM), jnp.bfloat16),
             pltpu.VMEM((HEADS, CHUNK, DIM), jnp.bfloat16),
             pltpu.VMEM((2, FLAG_ROWS, TILE), jnp.float32),
-            pltpu.VMEM((2, FLAG_ROWS, KEYS), jnp.float32),
+            pltpu.VMEM((HEADS * TILES + 2, KEYS), jnp.float32),
+            pltpu.VMEM((CHUNK // PAIR, PAIR, KEYS), jnp.float32),
             dma, dma, dma((2,)), dma, dma((4,)),
-            dma((HEADS,)), dma((HEADS,)), dma, dma, dma((2, HEADS)), dma((2, HEADS)),
+            dma((UNITS,)), dma((HEADS,)), dma, dma, dma((2, UNITS)), dma((2, UNITS)),
         ],
         compiler_params=pltpu.CompilerParams(
-            collective_id=0, has_side_effects=True, vmem_limit_bytes=48 * 1024 * 1024
+            collective_id=0, has_side_effects=True, vmem_limit_bytes=56 * 1024 * 1024
         ),
     )(query_rows, key_rows, value_rows, flags)
 

time: 178 us -> 124 us (0.70)
  Pallas kernels: 171 us -> 115 us
  between operations: 0.06 us -> 1.89 us
    pallas_call x1, Pallas kernels: 171 us -> 115 us  [per_device(): pl.pallas_call(kernel, out_shape=jax.ShapeDtypeStruct(query_rows.shape, j...]
    unnamed x9 -> x5, local copies, waits for them, and re-layouts: 4.55 us -> 2.77 us
where the time goes in v2:
time: 124 us; the launch traced here: 122 us
  Pallas kernels  115 us (93%)
  local copies, waits for them, and re-layouts  3.63 us (3%)
  between operations  1.89 us (2%)
    pallas_call x1, Pallas kernels, per_device(): pl.pallas_call(kernel, out_shape=jax.ShapeDtypeStruct(query_rows.shape, j...  115 us
    unnamed x5, local copies, waits for them, and re-layouts  2.77 us

profile of v2, /device:TPU:11, one launch (start us, length us, event | category | flops | bytes accessed | tf_op | source)
XLA Modules:
  0.0 121.7 jit_solution(5370075182171250783)
XLA Ops:
  0.0 0.0 copy-start.1
  0.0 0.0 copy-start
  0.0 0.1 broadcast_compare_fusion
  0.1 0.6 copy-done.1
  0.7 0.1 le.24
  0.7 0.1 subtract_abs_fusion
  0.8 0.6 fusion.2
  3.2 0.1 le.25
  3.3 0.1 le.26
  3.4 0.0 copy-done
  3.4 0.2 broadcast_select_fusion.2
  3.7 0.1 compare_and_fusion
  3.8 0.6 pad_convert_fusion.flag_ref
  4.4 115.2 %shard_map.55 = bf16[96,5120]{1,0:T(8,128)(2,1)} custom-call(bf16[96,5120]{1,0:T(8,128)(2,1)} %q_ref.1, bf16[96,5120]{1,0:T(8,128)(2,1)} %k_ref.1, bf16[96,5120]{1,0:T(8,128)(2,1)} %v_ref.1, f32[2,16,128]{2,1,0:T(8,128)} %pad_convert_fusion.flag_ref), custom_call_target="tpu_custom_call" | custom-call | tf_op jit(solution)/shard_map/pallas_call | solution.py:342
  119.5 2.2 %copy.7 = bf16[96,5120]{1,0:T(8,128)(2,1)} copy(bf16[96,5120]{1,0:T(8,128)(2,1)} %shard_map.55) | data formatting | bytes 1966080
  (7 shorter events, 0.1 us)
Async XLA Ops:
  0.0 0.7 copy-start.1
  0.0 3.4 %copy-start = (s32[10,3,192]{2,1,0:T(4,128)S(1)}, s32[10,3,192]{2,1,0:T(4,128)}, u32[]{:S(2)}) copy-start(s32[10,3,192]{2,1,0:T(4,128)} %param.8) | copy-start | bytes 69124

commit v3 on v2

v3 whole, which is shorter than its diff:
```python
import math

import jax
import jax.numpy as jnp
from jax import lax
from jax.experimental import pallas as pl
from jax.experimental.pallas import tpu as pltpu
from jax.sharding import PartitionSpec as P

MESH = pl.DeviceIdType.MESH
TILE = 128
DIM = 128
HEADS = 5
ROWS = 96
CHUNK = 768
TILES = CHUNK // TILE
REACH = 12
NEAR = 3
PAIR = 2 * TILE
SPAN = 2 * REACH + 2
KEYS = SPAN * TILE
STEP = 256
UNITS = 2 * HEADS
PIECES = 3 * HEADS
FIRST = 2
LEAD = 3
WINDOW = 5 * CHUNK
OWN = 2 * CHUNK
CHUNKS = 32
RING = 4
FLAG_ROWS = 16
COUNT = 192
LOW = 1e30
RATE = math.log2(math.e) / math.sqrt(DIM)


def wait_for(ref, sem):
    pltpu.make_async_copy(ref, ref, sem).wait()


def kernel(
    q_ref, k_ref, v_ref, mask_ref, type_ref, o_ref,
    kv, qb, ob, masks, lines, shown, flags, bias, held, weights, totals,
    mask_copy, kv_send, q_send, flag_send, o_send, y_send,
    kv_recv, q_recv, flag_recv, o_recv, near_recv, far_recv,
):
    hd = lax.axis_index("head")
    ctx = lax.axis_index("ctx")
    zh = ctx // 32
    xy = (ctx // 2) % 16
    core = ctx % 2
    z = zh * 4 + hd
    chunk = core * 16 + xy
    loops = zh == core
    has_left = chunk > 0
    has_right = chunk < CHUNKS - 1

    def at(z_, xy_, core_):
        return {"head": z_ % 4, "ctx": (z_ // 4) * 32 + xy_ * 2 + core_}

    def beside(by):
        other = (chunk + by + CHUNKS) % CHUNKS
        return at(z, other % 16, other // 16)

    left, right = beside(-1), beside(1)
    back, ahead = beside(-RING), beside(RING)
    y = xy % RING
    first_row = chunk < RING
    last_row = chunk >= CHUNKS - RING
    at_start, at_end = y == 0, y == RING - 1
    inside = jnp.logical_not(jnp.logical_or(at_start, at_end))
    closing = beside(jnp.where(at_start, RING - 1, 1 - RING))

    barrier = pltpu.get_barrier_semaphore()

    def greet(n, carry):
        other = (z * 2 + core + n) % 16
        pl.semaphore_signal(barrier, inc=1, device_id=at(other // 2, xy, other % 2), device_id_type=MESH)
        return carry

    lax.fori_loop(1, 16, greet, 0)

    has_back, has_ahead = jnp.logical_not(first_row), jnp.logical_not(last_row)
    has_closing = jnp.logical_not(inside)
    partners = ((has_left, left), (has_right, right), (has_back, back), (has_ahead, ahead), (has_closing, closing))
    for there, partner in partners:

        @pl.when(there)
        def _():
            pl.semaphore_signal(barrier, inc=1, device_id=partner, device_id_type=MESH)

    pl.semaphore_wait(barrier, 15 + sum(there.astype(jnp.int32) for there, _ in partners))

    mine = core * 384 + hd * ROWS

    fetch = pltpu.make_async_copy(mask_ref, masks, mask_copy)
    fetch.start()

    def parts(i, z_):
        cols = pl.ds(pl.multiple_of((z_ * HEADS + i) * DIM, DIM), DIM)
        rows = pl.ds(pl.multiple_of(OWN + mine, 16), ROWS)
        q_rows = pl.ds(pl.multiple_of(mine, 16), ROWS)
        return (
            (k_ref.at[:, cols], kv.at[2 * i, rows, :], kv_send.at[2 * i], kv_recv.at[2 * i]),
            (v_ref.at[:, cols], kv.at[2 * i + 1, rows, :], kv_send.at[2 * i + 1], kv_recv.at[2 * i + 1]),
            (q_ref.at[:, cols], qb.at[i, q_rows, :], q_send, q_recv.at[i]),
        )

    def push(src, dst, send, recv, to):
        pltpu.make_async_remote_copy(
            src_ref=src, dst_ref=dst, send_sem=send, recv_sem=recv, device_id=to, device_id_type=MESH
        ).start()

    def spread(i, kind):
        def one(j, carry):
            half = j // 2 + 1
            step = jnp.where(j % 2 == 0, half, 8 - half)
            z_ = (z + step) % 8
            src, dst, send, recv = parts(i, z_)[kind]
            push(src, dst, send, recv, at(z_, xy, zh))
            return carry

        lax.fori_loop(0, 7, one, 0)

        @pl.when(loops)
        def _():
            src, dst, send, recv = parts(i, z)[kind]
            pltpu.make_async_copy(src, dst, recv).start()

        @pl.when(jnp.logical_not(loops))
        def _():
            src, dst, send, recv = parts(i, z)[kind]
            push(src, dst, send, recv, at(z, xy, zh))

    def issue(n, carry):
        late = n - 6
        turn, third = late // 3, late % 3
        i = jnp.where(n < 6, n // 2, jnp.where(n < 12, jnp.where(third == 0, turn, turn + 3), n - 10))
        kind = jnp.where(n < 6, n % 2, jnp.where(jnp.logical_and(n < 12, third > 0), third - 1, 2))
        for option in range(3):

            @pl.when(kind == option)
            def _():
                spread(i, option)

        return carry

    def left_here(u):
        @pl.when(loops)
        def _():
            wait_for(kv.at[u, pl.ds(0, CHUNK - ROWS), :], kv_send.at[u])

        @pl.when(jnp.logical_not(loops))
        def _():
            wait_for(kv.at[u, pl.ds(0, CHUNK), :], kv_send.at[u])

    issue(0, 0)
    left_here(0)
    lax.fori_loop(1, FIRST, issue, 0)

    fetch.wait()
    lines[...] = jnp.zeros_like(lines)
    for h in range(2 * HEADS):
        row = (h // HEADS) * FLAG_ROWS + (h % HEADS) * 3
        lines[pl.ds(row, 3), pl.ds(0, COUNT)] = jnp.where(masks[h] == 1, 1.0, 0.0)
    shape = (2 * FLAG_ROWS, TILE)
    row = lax.broadcasted_iota(jnp.int32, shape, 0)
    third = (row % FLAG_ROWS) % 3
    head_ = (row // FLAG_ROWS) * HEADS + (row % FLAG_ROWS) // 3
    limit = jnp.full(shape, NEAR, jnp.int32)
    for h in range(2 * HEADS):
        limit = jnp.where(jnp.logical_and(head_ == h, type_ref[h] == 1), REACH, limit)
    allowed = jnp.zeros(shape, jnp.float32)
    pick_row = lax.broadcasted_iota(jnp.int32, (lines.shape[1], TILE), 0)
    pick_col = lax.broadcasted_iota(jnp.int32, (lines.shape[1], TILE), 1)
    col = lax.broadcasted_iota(jnp.int32, shape, 1)
    for t in range(3):
        shift = (ctx + t) % 2
        pick = (pick_row - pick_col == 3 * ctx + t - shift - REACH).astype(jnp.bfloat16)
        seen = jnp.dot(lines[...].astype(jnp.bfloat16), pick, preferred_element_type=jnp.float32)
        distance = jnp.abs(col - shift - REACH)
        seen = jnp.where(distance == 0, 1.0, jnp.where(distance <= limit, seen, 0.0))
        allowed = jnp.where(third == t, seen, allowed)
    for e in range(2):
        shown[e] = allowed[e * FLAG_ROWS : (e + 1) * FLAG_ROWS]

    for e in range(2):
        z_ = 2 * hd + e
        here = jnp.logical_and(loops, z_ == z)

        @pl.when(here)
        def _():
            pltpu.make_async_copy(shown.at[e], flags.at[core], flag_recv).start()

        @pl.when(jnp.logical_not(here))
        def _():
            push(shown.at[e], flags.at[core], flag_send.at[e], flag_recv, at(z_, xy, zh))

    def clear(slot, when):
        @pl.when(when)
        def _():
            def one(i, carry):
                kv[i, pl.ds(slot * CHUNK, CHUNK), :] = jnp.zeros((CHUNK, DIM), jnp.bfloat16)
                return carry

            lax.fori_loop(0, UNITS, one, 0)

    clear(0, chunk < 2)
    clear(1, chunk < 1)
    clear(3, chunk > CHUNKS - 2)
    clear(4, chunk > CHUNKS - 3)

    def slot(i, s):
        return kv.at[i, pl.ds(s * CHUNK, CHUNK), :]

    def send_own(i):
        wait_for(slot(i, 2), kv_recv.at[i])

        @pl.when(has_right)
        def _():
            push(slot(i, 2), slot(i, 1), y_send.at[0], near_recv.at[0, i], right)

        @pl.when(has_left)
        def _():
            push(slot(i, 2), slot(i, 3), y_send.at[1], near_recv.at[1, i], left)

    def both(*terms):
        out = terms[0]
        for term in terms[1:]:
            out = jnp.logical_and(out, term)
        return out

    def either(one, other):
        return jnp.logical_or(one, other)

    to_right = (both(inside, has_left), both(has_left, either(at_start, both(y == 1, first_row))))
    to_left = (both(inside, has_right), both(has_right, either(at_end, both(y == 2, last_row))))
    left_closes = both(at_end, has_left)
    right_closes = both(at_start, has_right)
    high_first = (y < 2, y % 2 == 0)
    has_low, has_high = chunk >= 2, chunk < CHUNKS - 2

    def pass_on(u, kind):
        @pl.when(has_left)
        def _():
            wait_for(slot(u, 1), near_recv.at[0, u])

        @pl.when(to_right[kind])
        def _():
            push(slot(u, 1), slot(u, 0), y_send.at[2 + kind], far_recv.at[0, u], right)

        if kind == 1:

            @pl.when(left_closes)
            def _():
                push(slot(u, 1), slot(u, 4), y_send.at[6], far_recv.at[1, u], closing)

        @pl.when(has_right)
        def _():
            wait_for(slot(u, 3), near_recv.at[1, u])

        @pl.when(to_left[kind])
        def _():
            push(slot(u, 3), slot(u, 4), y_send.at[4 + kind], far_recv.at[1, u], left)

        if kind == 1:

            @pl.when(right_closes)
            def _():
                push(slot(u, 3), slot(u, 0), y_send.at[7], far_recv.at[0, u], closing)

    def pass_across(u, kind):
        high = high_first[kind]

        @pl.when(both(high, has_high))
        def _():
            wait_for(slot(u, 4), far_recv.at[1, u])

        @pl.when(both(high, has_ahead))
        def _():
            push(slot(u, 4), slot(u, 0), y_send.at[8 + kind], far_recv.at[0, u], ahead)

        @pl.when(both(jnp.logical_not(high), has_low))
        def _():
            wait_for(slot(u, 0), far_recv.at[0, u])

        @pl.when(both(jnp.logical_not(high), has_back))
        def _():
            push(slot(u, 0), slot(u, 4), y_send.at[10 + kind], far_recv.at[1, u], back)

    def see():
        wait_for(flags, flag_recv)
        spots = lax.broadcasted_iota(jnp.int32, (TILE, KEYS), 1) // TILE
        rows_ = lax.broadcasted_iota(jnp.int32, (TILE, KEYS), 0)
        wide = (spots == rows_).astype(jnp.bfloat16)
        for c in range(2):
            seen = jnp.dot(flags[c].astype(jnp.bfloat16), wide, preferred_element_type=jnp.float32)
            seen = (seen - 1.0) * LOW
            for i in range(HEADS):
                bias[pl.ds(i * TILES + 3 * c, 3), :] = seen[3 * i : 3 * i + 3]

    def attend(i):
        def arrived(u, kind):
            @pl.when(both(high_first[kind], has_low))
            def _():
                wait_for(slot(u, 0), far_recv.at[0, u])

            @pl.when(both(jnp.logical_not(high_first[kind]), has_high))
            def _():
                wait_for(slot(u, 4), far_recv.at[1, u])

        wait_for(qb.at[i], q_recv.at[i])
        arrived(2 * i, 0)
        for p in range(CHUNK // PAIR):
            start = p * PAIR
            q = qb[i, pl.ds(start, PAIR), :]
            best = jnp.full((PAIR, TILE), -3e38, jnp.float32)
            for j in range(0, KEYS, STEP):
                keys = kv[2 * i, pl.ds(start + j, STEP), :]
                s = lax.dot_general(q, keys, (((1,), (1,)), ((), ())), preferred_element_type=jnp.float32)
                even = s[:TILE] + bias[pl.ds(i * TILES + 2 * p, 1), pl.ds(j, STEP)]
                odd = s[TILE:] + bias[pl.ds(i * TILES + 2 * p + 1, 1), pl.ds(j, STEP)]
                s = jnp.concatenate([even, odd], axis=0)
                held[p, :, pl.ds(j, STEP)] = s
                for t in range(0, STEP, TILE):
                    best = jnp.maximum(best, s[:, t : t + TILE])
            best = jnp.max(best, axis=1, keepdims=True)
            total = jnp.zeros((PAIR, TILE), jnp.float32)
            for j in range(0, KEYS, STEP):
                raw = jnp.exp2((held[p, :, pl.ds(j, STEP)] - best) * RATE)
                for t in range(0, STEP, TILE):
                    total = total + raw[:, t : t + TILE]
                weights[p, :, pl.ds(j, STEP)] = raw.astype(jnp.bfloat16)
            totals[p] = jnp.broadcast_to(jnp.sum(total, axis=1, keepdims=True), (PAIR, TILE))

        arrived(2 * i + 1, 1)
        for p in range(CHUNK // PAIR):
            start = p * PAIR
            values = kv[2 * i + 1, pl.ds(start, KEYS), :]
            mixed = jnp.dot(weights[p], values, preferred_element_type=jnp.float32)
            ob[i, pl.ds(start, PAIR), :] = (mixed / totals[p]).astype(jnp.bfloat16)

        cols = pl.ds(pl.multiple_of((z * HEADS + i) * DIM, DIM), DIM)

        def owner(n):
            zl = (hd + n // 2) % 4
            cs = (core + n) % 2
            return ob.at[i, pl.ds(pl.multiple_of(cs * 384 + zl * ROWS, 16), ROWS), :], at(core * 4 + zl, xy, cs)

        @pl.when(loops)
        def _():
            pltpu.make_async_copy(owner(0)[0], o_ref.at[:, cols], o_recv).start()

        @pl.when(jnp.logical_not(loops))
        def _():
            push(owner(0)[0], o_ref.at[:, cols], o_send, o_recv, owner(0)[1])

        def one(n, carry):
            src, to = owner(n)
            push(src, o_ref.at[:, cols], o_send, o_recv, to)
            return carry

        lax.fori_loop(1, 8, one, 0)

    def advance(s, carry):
        @pl.when(s < HEADS)
        def _():
            for t in range(2):
                u = 2 * s + t
                send_own(u)
                low = jnp.where(u == 0, FIRST, jnp.minimum(PIECES, LEAD + 2 * u - 2))
                lax.fori_loop(low, jnp.minimum(PIECES, LEAD + 2 * u), issue, 0)

                @pl.when(u > 0)
                def _():
                    pass_on(u - 1, 1 - t)

                @pl.when(u > 1)
                def _():
                    pass_across(u - 2, t)

            @pl.when(s == 0)
            def _():
                see()

        @pl.when(s == HEADS)
        def _():
            pass_on(UNITS - 1, 1)
            pass_across(UNITS - 2, 0)

        @pl.when(s == HEADS + 1)
        def _():
            pass_across(UNITS - 1, 1)

        @pl.when(s >= 2)
        def _():
            attend(s - 2)

        return carry

    lax.fori_loop(0, HEADS + 2, advance, 0)

    wait_for(o_ref, o_recv)

    def sent(rows):
        wait_for(qb.at[:, pl.ds(0, rows), :], q_send)
        wait_for(ob.at[:, pl.ds(0, rows), :], o_send)

    @pl.when(loops)
    def _():
        sent(CHUNK - ROWS)

    @pl.when(jnp.logical_not(loops))
    def _():
        sent(CHUNK)

    def drain(u, carry):
        left_here(u)
        return carry

    lax.fori_loop(1, UNITS, drain, 0)

    for e in range(2):

        @pl.when(jnp.logical_not(jnp.logical_and(loops, 2 * hd + e == z)))
        def _():
            wait_for(shown.at[e], flag_send.at[e])

    gone = [(has_right, 0, UNITS), (has_left, 1, UNITS), (left_closes, 6, HEADS), (right_closes, 7, HEADS)]
    for kind in range(2):
        gone += [(to_right[kind], 2 + kind, HEADS), (to_left[kind], 4 + kind, HEADS)]
        gone += [(both(high_first[kind], has_ahead), 8 + kind, HEADS)]
        gone += [(both(jnp.logical_not(high_first[kind]), has_back), 10 + kind, HEADS)]
    for there, which, units in gone:

        @pl.when(there)
        def _():
            wait_for(kv.at[pl.ds(0, units), pl.ds(0, CHUNK), :], y_send.at[which])


def per_device(query_rows, key_rows, value_rows, block_mask, head_type):
    any_ = pl.BlockSpec(memory_space=pltpu.HBM)
    dma = pltpu.SemaphoreType.DMA
    return pl.pallas_call(
        kernel,
        out_shape=jax.ShapeDtypeStruct(query_rows.shape, jnp.bfloat16),
        in_specs=[any_] * 4 + [pl.BlockSpec(memory_space=pltpu.SMEM)],
        out_specs=pl.BlockSpec(memory_space=pltpu.VMEM),
        scratch_shapes=[
            pltpu.VMEM((UNITS, WINDOW, DIM), jnp.bfloat16),
            pltpu.VMEM((HEADS, CHUNK, DIM), jnp.bfloat16),
            pltpu.VMEM((HEADS, CHUNK, DIM), jnp.bfloat16),
            pltpu.VMEM(block_mask.shape, jnp.int32),
            pltpu.VMEM((2 * FLAG_ROWS, 2 * TILE), jnp.float32),
            pltpu.VMEM((2, FLAG_ROWS, TILE), jnp.float32),
            pltpu.VMEM((2, FLAG_ROWS, TILE), jnp.float32),
            pltpu.VMEM((HEADS * TILES + 2, KEYS), jnp.float32),
            pltpu.VMEM((CHUNK // PAIR, PAIR, KEYS), jnp.float32),
            pltpu.VMEM((CHUNK // PAIR, PAIR, KEYS), jnp.bfloat16),
            pltpu.VMEM((CHUNK // PAIR, PAIR, TILE), jnp.float32),
            dma, dma((UNITS,)), dma, dma((2,)), dma, dma((12,)),
            dma((UNITS,)), dma((HEADS,)), dma, dma, dma((2, UNITS)), dma((2, UNITS)),
        ],
        compiler_params=pltpu.CompilerParams(
            collective_id=0, has_side_effects=True, vmem_limit_bytes=56 * 1024 * 1024
        ),
    )(query_rows, key_rows, value_rows, block_mask, head_type)


def solution(mesh):
    placed = (
        P(("ctx", "head"), None),
        P(("ctx", "head"), None),
        P(("ctx", "head"), None),
        P("head", "ctx", None),
        P("head"),
    )
    return jax.shard_map(
        per_device, mesh=mesh, in_specs=placed, out_specs=P(("ctx", "head"), None), check_vma=False
    )
```

time: 124 us -> 125 us (level)
  Pallas kernels: 115 us -> 120 us
  between operations: 1.89 us -> 0.01 us
  local copies, waits for them, and re-layouts: 3.63 us -> 2.21 us
    pallas_call x1, Pallas kernels: 115 us -> 120 us  [per_device(): pl.pallas_call(kernel, out_shape=jax.ShapeDtypeStruct(query_rows.shape, j...]
    unnamed x5 -> x1, local copies, waits for them, and re-layouts: 2.77 us -> 2.21 us
where the time goes in v3:
time: 125 us; the launch traced here: 123 us
  Pallas kernels  120 us (96%)
  local copies, waits for them, and re-layouts  2.21 us (2%)
    pallas_call x1, Pallas kernels, per_device(): pl.pallas_call(kernel, out_shape=jax.ShapeDtypeStruct(query_rows.shape, j...  120 us

profile of v3, /device:TPU:11, one launch (start us, length us, event | category | flops | bytes accessed | tf_op | source)
XLA Modules:
  0.0 122.7 jit_solution(16169306489965820520)
XLA Ops:
  0.0 120.5 %shard_map.55 = bf16[96,5120]{1,0:T(8,128)(2,1)} custom-call(bf16[96,5120]{1,0:T(8,128)(2,1)} %q_ref.1, bf16[96,5120]{1,0:T(8,128)(2,1)} %k_ref.1, bf16[96,5120]{1,0:T(8,128)(2,1)} %v_ref.1, s32[10,3,192]{2,1,0:T(4,128)} %mask_ref.1, s32[10]{0:T(128)} %type_ref.1), custom_call_target="tpu_custom_call" | custom-call | tf_op jit(solution)/shard_map/pallas_call | solution.py:444
  120.5 2.2 %copy.7 = bf16[96,5120]{1,0:T(8,128)(2,1)} copy(bf16[96,5120]{1,0:T(8,128)(2,1)} %shard_map.55) | data formatting | bytes 1966080

commit v4 on v3

--- a/solution.py
+++ b/solution.py
@@ -23,7 +23,9 @@
 UNITS = 2 * HEADS
 PIECES = 3 * HEADS
 FIRST = 2
-LEAD = 3
+LAG_ON, LAG_ACROSS = 1, 3
+LAG_ATTEND, TURN = 2, 1
+LEAD = 7
 WINDOW = 5 * CHUNK
 OWN = 2 * CHUNK
 CHUNKS = 32
@@ -362,43 +364,40 @@
 
         lax.fori_loop(1, 8, one, 0)
 
+    def within(n, count):
+        return jnp.logical_and(n >= 0, n < count)
+
     def advance(s, carry):
-        @pl.when(s < HEADS)
-        def _():
-            for t in range(2):
-                u = 2 * s + t
+        for t in range(2):
+            u = 2 * s + t
+
+            @pl.when(u < UNITS)
+            def _():
                 send_own(u)
                 low = jnp.where(u == 0, FIRST, jnp.minimum(PIECES, LEAD + 2 * u - 2))
                 lax.fori_loop(low, jnp.minimum(PIECES, LEAD + 2 * u), issue, 0)
 
-                @pl.when(u > 0)
+            @pl.when(within(u - LAG_ON, UNITS))
+            def _():
+                pass_on(u - LAG_ON, (t - LAG_ON) % 2)
+
+            @pl.when(within(u - LAG_ACROSS, UNITS))
+            def _():
+                pass_across(u - LAG_ACROSS, (t - LAG_ACROSS) % 2)
+
+            if t == TURN:
+
+                @pl.when(s == 0)
                 def _():
-                    pass_on(u - 1, 1 - t)
-
-                @pl.when(u > 1)
+                    see()
+
+                @pl.when(within(s - LAG_ATTEND, HEADS))
                 def _():
-                    pass_across(u - 2, t)
-
-            @pl.when(s == 0)
-            def _():
-                see()
-
-        @pl.when(s == HEADS)
-        def _():
-            pass_on(UNITS - 1, 1)
-            pass_across(UNITS - 2, 0)
-
-        @pl.when(s == HEADS + 1)
-        def _():
-            pass_across(UNITS - 1, 1)
-
-        @pl.when(s >= 2)
-        def _():
-            attend(s - 2)
+                    attend(s - LAG_ATTEND)
 
         return carry
 
-    lax.fori_loop(0, HEADS + 2, advance, 0)
+    lax.fori_loop(0, HEADS + LAG_ATTEND, advance, 0)
 
     wait_for(o_ref, o_recv)
 
@@ -443,9 +442,9 @@
     dma = pltpu.SemaphoreType.DMA
     return pl.pallas_call(
         kernel,
-        out_shape=jax.ShapeDtypeStruct(query_rows.shape, jnp.bfloat16),
+        out_shape=pltpu.VMEM(query_rows.shape, jnp.bfloat16),
         in_specs=[any_] * 4 + [pl.BlockSpec(memory_space=pltpu.SMEM)],
-        out_specs=pl.BlockSpec(memory_space=pltpu.VMEM),
+        out_specs=pl.BlockSpec(memory_space=pl.ANY),
         scratch_shapes=[
             pltpu.VMEM((UNITS, WINDOW, DIM), jnp.bfloat16),
             pltpu.VMEM((HEADS, CHUNK, DIM), jnp.bfloat16),

time: 125 us -> 107 us (0.86); the launches traced: 123 us -> 107 us
  Pallas kernels: 120 us -> 106 us
  local copies, waits for them, and re-layouts: 2.21 us -> 0.95 us
    pallas_call x1, Pallas kernels: 120 us -> 106 us  [per_device(): pl.pallas_call(kernel, out_shape=pltpu.VMEM(query_rows.shape, jnp.bfloat1...]
    unnamed x1, local copies, waits for them, and re-layouts: 2.21 us -> 0.95 us
where the time goes in v4:
time: 107 us
  Pallas kernels  106 us (99%)
    pallas_call x1, Pallas kernels, per_device(): pl.pallas_call(kernel, out_shape=pltpu.VMEM(query_rows.shape, jnp.bfloat1...  106 us

profile of v4, /device:TPU:11, one launch (start us, length us, event | category | flops | bytes accessed | tf_op | source)
XLA Modules:
  0.0 106.9 jit_solution(9216590302934845530)
XLA Ops:
  0.0 105.9 %shard_map.55 = bf16[96,5120]{1,0:T(8,128)(2,1)S(1)} custom-call(bf16[96,5120]{1,0:T(8,128)(2,1)} %q_ref.1, bf16[96,5120]{1,0:T(8,128)(2,1)} %k_ref.1, bf16[96,5120]{1,0:T(8,128)(2,1)} %v_ref.1, s32[10,3,192]{2,1,0:T(4,128)} %mask_ref.1, s32[10]{0:T(128)} %type_ref.1), custom_call_target="tpu_custom_call" | custom-call | tf_op jit(solution)/shard_map/pallas_call | solution.py:443
  105.9 0.9 copy.7

commit v5 on v4

--- a/solution.py
+++ b/solution.py
@@ -24,8 +24,8 @@
 PIECES = 3 * HEADS
 FIRST = 2
 LAG_ON, LAG_ACROSS = 1, 3
-LAG_ATTEND, TURN = 2, 1
-LEAD = 7
+START, LATE = 5, 13
+AHEAD = 4
 WINDOW = 5 * CHUNK
 OWN = 2 * CHUNK
 CHUNKS = 32
@@ -157,8 +157,6 @@
             wait_for(kv.at[u, pl.ds(0, CHUNK), :], kv_send.at[u])
 
     issue(0, 0)
-    left_here(0)
-    lax.fori_loop(1, FIRST, issue, 0)
 
     fetch.wait()
     lines[...] = jnp.zeros_like(lines)
@@ -198,6 +196,9 @@
         def _():
             push(shown.at[e], flags.at[core], flag_send.at[e], flag_recv, at(z_, xy, zh))
 
+    left_here(0)
+    lax.fori_loop(1, FIRST, issue, 0)
+
     def clear(slot, when):
         @pl.when(when)
         def _():
@@ -234,6 +235,9 @@
 
     def either(one, other):
         return jnp.logical_or(one, other)
+
+    def way(kind, keys, values):
+        return either(both(kind == 0, keys), both(kind == 1, values))
 
     to_right = (both(inside, has_left), both(has_left, either(at_start, both(y == 1, first_row))))
     to_left = (both(inside, has_right), both(has_right, either(at_end, both(y == 2, last_row))))
@@ -247,32 +251,28 @@
         def _():
             wait_for(slot(u, 1), near_recv.at[0, u])
 
-        @pl.when(to_right[kind])
+        @pl.when(way(kind, *to_right))
         def _():
             push(slot(u, 1), slot(u, 0), y_send.at[2 + kind], far_recv.at[0, u], right)
 
-        if kind == 1:
-
-            @pl.when(left_closes)
-            def _():
-                push(slot(u, 1), slot(u, 4), y_send.at[6], far_recv.at[1, u], closing)
+        @pl.when(both(kind == 1, left_closes))
+        def _():
+            push(slot(u, 1), slot(u, 4), y_send.at[6], far_recv.at[1, u], closing)
 
         @pl.when(has_right)
         def _():
             wait_for(slot(u, 3), near_recv.at[1, u])
 
-        @pl.when(to_left[kind])
+        @pl.when(way(kind, *to_left))
         def _():
             push(slot(u, 3), slot(u, 4), y_send.at[4 + kind], far_recv.at[1, u], left)
 
-        if kind == 1:
-
-            @pl.when(right_closes)
-            def _():
-                push(slot(u, 3), slot(u, 0), y_send.at[7], far_recv.at[0, u], closing)
+        @pl.when(both(kind == 1, right_closes))
+        def _():
+            push(slot(u, 3), slot(u, 0), y_send.at[7], far_recv.at[0, u], closing)
 
     def pass_across(u, kind):
-        high = high_first[kind]
+        high = way(kind, *high_first)
 
         @pl.when(both(high, has_high))
         def _():
@@ -364,40 +364,39 @@
 
         lax.fori_loop(1, 8, one, 0)
 
+    def place(u):
+        return u + jnp.where(u >= 6, 1, 0) + jnp.where(u >= 8, 1, 0)
+
     def within(n, count):
         return jnp.logical_and(n >= 0, n < count)
 
-    def advance(s, carry):
-        for t in range(2):
-            u = 2 * s + t
-
-            @pl.when(u < UNITS)
-            def _():
-                send_own(u)
-                low = jnp.where(u == 0, FIRST, jnp.minimum(PIECES, LEAD + 2 * u - 2))
-                lax.fori_loop(low, jnp.minimum(PIECES, LEAD + 2 * u), issue, 0)
-
-            @pl.when(within(u - LAG_ON, UNITS))
-            def _():
-                pass_on(u - LAG_ON, (t - LAG_ON) % 2)
-
-            @pl.when(within(u - LAG_ACROSS, UNITS))
-            def _():
-                pass_across(u - LAG_ACROSS, (t - LAG_ACROSS) % 2)
-
-            if t == TURN:
-
-                @pl.when(s == 0)
-                def _():
-                    see()
-
-                @pl.when(within(s - LAG_ATTEND, HEADS))
-                def _():
-                    attend(s - LAG_ATTEND)
+    def advance(u, carry):
+        @pl.when(u < UNITS)
+        def _():
+            send_own(u)
+            low = jnp.where(u == 0, FIRST, jnp.minimum(PIECES, place(u - 1) + AHEAD))
+            high = jnp.where(u == UNITS - 1, PIECES, jnp.minimum(PIECES, place(u) + AHEAD))
+            lax.fori_loop(low, high, issue, 0)
+
+        @pl.when(within(u - LAG_ON, UNITS))
+        def _():
+            pass_on(u - LAG_ON, (u - LAG_ON) % 2)
+
+        @pl.when(within(u - LAG_ACROSS, UNITS))
+        def _():
+            pass_across(u - LAG_ACROSS, (u - LAG_ACROSS) % 2)
+
+        @pl.when(u == 1)
+        def _():
+            see()
+
+        @pl.when(jnp.logical_and(u >= START, either(u >= LATE, (u - START) % 2 == 0)))
+        def _():
+            attend(jnp.where(u >= LATE, u - LATE + (LATE - START + 1) // 2, (u - START) // 2))
 
         return carry
 
-    lax.fori_loop(0, HEADS + LAG_ATTEND, advance, 0)
+    lax.fori_loop(0, LATE + HEADS - (LATE - START + 1) // 2, advance, 0)
 
     wait_for(o_ref, o_recv)
 

time: 107 us -> 116 us (1.084)
  Pallas kernels: 106 us -> 114 us
    pallas_call x1, Pallas kernels: 106 us -> 114 us  [per_device(): pl.pallas_call(kernel, out_shape=pltpu.VMEM(query_rows.shape, jnp.bfloat1...]
where the time goes in v5:
time: 116 us; the launch traced here: 115 us
  Pallas kernels  114 us (98%)
    pallas_call x1, Pallas kernels, per_device(): pl.pallas_call(kernel, out_shape=pltpu.VMEM(query_rows.shape, jnp.bfloat1...  114 us

profile of v5, /device:TPU:11, one launch (start us, length us, event | category | flops | bytes accessed | tf_op | source)
XLA Modules:
  0.0 115.2 jit_solution(9748117726047103329)
XLA Ops:
  0.0 114.3 %shard_map.55 = bf16[96,5120]{1,0:T(8,128)(2,1)S(1)} custom-call(bf16[96,5120]{1,0:T(8,128)(2,1)} %q_ref.1, bf16[96,5120]{1,0:T(8,128)(2,1)} %k_ref.1, bf16[96,5120]{1,0:T(8,128)(2,1)} %v_ref.1, s32[10,3,192]{2,1,0:T(4,128)} %mask_ref.1, s32[10]{0:T(128)} %type_ref.1), custom_call_target="tpu_custom_call" | custom-call | tf_op jit(solution)/shard_map/pallas_call | solution.py:442
  114.3 0.9 copy.7

commit v6 on v4

--- a/solution.py
+++ b/solution.py
@@ -25,7 +25,7 @@
 FIRST = 2
 LAG_ON, LAG_ACROSS = 1, 3
 LAG_ATTEND, TURN = 2, 1
-LEAD = 7
+LEAD = 10
 WINDOW = 5 * CHUNK
 OWN = 2 * CHUNK
 CHUNKS = 32

time: 107 us -> 107 us (level)
  no operation moved by 1% of the time
where the time goes in v6:
time: 107 us
  Pallas kernels  106 us (99%)
    pallas_call x1, Pallas kernels, per_device(): pl.pallas_call(kernel, out_shape=pltpu.VMEM(query_rows.shape, jnp.bfloat1...  106 us

profile of v6, /device:TPU:11, one launch (start us, length us, event | category | flops | bytes accessed | tf_op | source)
XLA Modules:
  0.0 106.9 jit_solution(4089616492108432130)
XLA Ops:
  0.0 105.9 %shard_map.55 = bf16[96,5120]{1,0:T(8,128)(2,1)S(1)} custom-call(bf16[96,5120]{1,0:T(8,128)(2,1)} %q_ref.1, bf16[96,5120]{1,0:T(8,128)(2,1)} %k_ref.1, bf16[96,5120]{1,0:T(8,128)(2,1)} %v_ref.1, s32[10,3,192]{2,1,0:T(4,128)} %mask_ref.1, s32[10]{0:T(128)} %type_ref.1), custom_call_target="tpu_custom_call" | custom-call | tf_op jit(solution)/shard_map/pallas_call | solution.py:443
  105.9 0.9 copy.7
